TPU v7x, 32 devices: a whole 2x2x4 slice. The times are simulated.
32 devices in a mesh: groups: 2 (over x), row: 16 (over z, y, core).
Axes of the slice: x: 2, y: 2, z: 4, core: 2. Of those that a mesh axis runs over, the one named last changes fastest.
Arguments:
- fine: bfloat16 [2048, 128, 128], P(('groups', 'row')), parts along dimension 0, may hold values from -6 to 6
- parent: bfloat16 [32, 256, 512], P(('groups', 'row')), parts along dimension 0, may hold values from -6 to 6
- coverage: int32 [64, 4], P('groups'), parts along dimension 0, may hold values from 0 to 15
- owner_slot: int32 [32], P('groups'), parts along dimension 0, may hold values from 0 to 15, each once
- w_query: bfloat16 [128, 128], replicated, may hold values from -0.5 to 0.5
- w_key: bfloat16 [512, 128], replicated, may hold values from -0.25 to 0.25
- w_value: bfloat16 [512, 128], replicated, may hold values from -0.25 to 0.25
- norm_gain: float32 [128], replicated, may hold values from 0.1 to 1.9
- conv_weight: bfloat16 [4, 3, 3, 128, 128], replicated, may hold values from -0.25 to 0.25
- conv_bias: float32 [4, 128], replicated, may hold values from -3 to 3
Outputs:
- refined: bfloat16 [2048, 128, 128], P(('groups', 'row')), parts along dimension 0
There are 2 independent parts, one for each index of `groups`. A program takes and returns all parts, laid end to end along the dimension named above; an argument that names none is the same for every part. Nothing has to cross between parts.
Inputs may be any that keep to these rules, and one draw needn't show every extreme that they name: `owner_slot`: each slot exactly once.
All inputs are finite; a program needn't handle non-finite values.
Results may differ from a plain program's by a relative error of at most 0.014.
Values may be sent and summed in bfloat16 or wider, within the bound.
A program may use at most 128 MiB of HBM per device.

v0:
```python
import functools

import jax
import jax.numpy as jnp
from jax import lax
from jax.experimental import pallas as pl
from jax.experimental.pallas import tpu as pltpu
from jax.sharding import PartitionSpec as P

SUB = 16
LOG2E = 1.4426950408889634
VMEM_LIMIT = 56 * 1024 * 1024


def attend_kernel(cover_n, eps, slots_ref, fine_ref, *refs):
    kv_refs = refs[:cover_n]
    gain_ref, out_ref, k_scr, v_scr = refs[cover_n:]
    chans = fine_ref.shape[2]
    key_rows = kv_refs[0].shape[1]

    @pl.when(pl.program_id(1) == 0)
    def _():
        v_scr[...] = jnp.ones_like(v_scr)
        for j in range(cover_n):
            rows = slice(j * key_rows, (j + 1) * key_rows)
            k_scr[:, rows] = kv_refs[j][0, :, :chans].T
            v_scr[rows, :chans] = kv_refs[j][0, :, chans:]

    rows, cols = fine_ref.shape[:2]
    cells = fine_ref[...].reshape(rows * cols, chans)
    half = rows * cols // 2
    for part in range(2):
        mine = cells[part * half : (part + 1) * half]
        scores = jnp.dot(mine, k_scr[...], preferred_element_type=jnp.float32)
        top = jnp.max(scores, axis=-1, keepdims=True)
        weights = jnp.exp2(scores - top).astype(jnp.bfloat16)
        summed = jnp.dot(weights, v_scr[...], preferred_element_type=jnp.float32)
        attended = summed[:, :chans] / summed[:, chans:]
        meansq = jnp.mean(attended * attended, axis=-1, keepdims=True)
        mixed = mine.astype(jnp.float32) + gain_ref[...] * attended * lax.rsqrt(meansq + eps)
        out_ref[part * rows // 2 : (part + 1) * rows // 2] = mixed.astype(jnp.bfloat16).reshape(
            rows // 2, cols, chans
        )


def attend(fine, all_kv, slots, gain, tile_cols):
    side, width, chans = fine.shape
    cover_n = slots.shape[0] // tile_cols
    key_rows = all_kv.shape[1]
    rows = 16
    cells = pl.BlockSpec((rows, width // tile_cols, chans), lambda k, i, slots: (i, k, 0))

    def kv_spec(j):
        return pl.BlockSpec(
            (1, key_rows, 2 * chans), lambda k, i, slots: (slots[k * cover_n + j], 0, 0)
        )

    return pl.pallas_call(
        functools.partial(attend_kernel, cover_n, 1e-06),
        grid_spec=pltpu.PrefetchScalarGridSpec(
            num_scalar_prefetch=1,
            grid=(tile_cols, side // rows),
            in_specs=[cells]
            + [kv_spec(j) for j in range(cover_n)]
            + [pl.BlockSpec((1, chans), lambda k, i, slots: (0, 0))],
            out_specs=cells,
            scratch_shapes=[
                pltpu.VMEM((chans, cover_n * key_rows), jnp.bfloat16),
                pltpu.VMEM((cover_n * key_rows, 2 * chans), jnp.bfloat16),
            ],
        ),
        out_shape=jax.ShapeDtypeStruct(fine.shape, jnp.bfloat16),
        compiler_params=pltpu.CompilerParams(vmem_limit_bytes=VMEM_LIMIT),
        name="attend",
    )(slots, fine, *([all_kv] * cover_n), gain.reshape(1, chans))


def edge_columns(first, last):
    lane = lax.broadcasted_iota(jnp.int32, first.shape, first.ndim - 2)
    axis = first.ndim - 2
    west = jnp.where(lane == 0, 0.0, pltpu.roll(last, 1, axis))
    east = jnp.where(lane == SUB - 1, 0.0, pltpu.roll(first, SUB - 1, axis))
    return west, east


def conv_kernel(
    ends_ref, north_ref, mid_ref, south_ref, w_ref, b_ref, out_ref, wide, state_a, state_b, flat
):
    layers, _, _, chans, _ = w_ref.shape
    side, width, _ = mid_ref.shape
    steps = width // SUB
    halo = north_ref.shape[0]
    batch = flat.shape[0] // width

    def put(dst, parity, pair, num, cells):
        west, east = edge_columns(cells[:, 0], cells[:, steps - 1])
        dst[parity, pl.ds(pair, num), 1 : steps + 1] = cells.astype(jnp.bfloat16)
        dst[parity, pl.ds(pair, num), 0] = west.astype(jnp.bfloat16)
        dst[parity, pl.ds(pair, num), steps + 1] = east.astype(jnp.bfloat16)

    def take_rows(src, src_row, pair, num):
        rows = src[pl.ds(src_row, 2 * num)].astype(jnp.float32)
        flat[0 : 2 * num * width] = rows.reshape(2 * num * width, chans)
        for parity in range(2):
            for p in range(num):
                base = (2 * p + parity) * width
                cells = jnp.stack(
                    [flat[pl.ds(base + i, SUB, stride=steps), :] for i in range(steps)]
                )
                put(state_a, parity, pair + p, 1, cells[None])

    take_rows(north_ref, 0, 0, halo // 2)
    take_rows(south_ref, 0, (halo + side) // 2, halo // 2)
    group = batch // 2

    @pl.loop(0, side // batch)
    def _(c):
        take_rows(mid_ref, c * batch, halo // 2 + c * group, group)

    for layer in range(layers):
        for dx in range(3):
            for r in range(4):
                for o in range(2):
                    dy = r - o
                    at = (dx * 4 + r) * chans
                    if 0 <= dy <= 2:
                        block = w_ref[layer, dy, dx] * jnp.bfloat16(0.5)
                    else:
                        block = jnp.zeros((chans, chans), jnp.bfloat16)
                    wide[layer, at : at + chans, o * chans : (o + 1) * chans] = block

    src, dst = state_a, state_b
    for layer in range(layers):
        pairs = (side + 2 * (halo - 1 - layer)) // 2
        trips = -(-pairs // 8)
        size = -(-pairs // trips)
        bias = b_ref[layer] * 0.5
        bias = jnp.concatenate([bias, bias])[None, :]
        last = layer == layers - 1

        def chunk(pair, num, slot):
            lhs = jnp.concatenate(
                [
                    src[parity, pl.ds(pair + off, num), dx : dx + steps].reshape(num * width, chans)
                    for dx in range(3)
                    for off in range(2)
                    for parity in range(2)
                ],
                axis=1,
            )
            h = jnp.dot(lhs, wide[layer], preferred_element_type=jnp.float32) + bias
            h = h + h * jnp.tanh(h)
            for parity in range(2):
                cells = h[:, parity * chans : (parity + 1) * chans].reshape(num, steps, SUB, chans)
                if not last:
                    put(dst, parity, pair, num, cells)
                    continue
                for p in range(num):
                    base = ((slot + p) * 2 + parity) * width
                    for i in range(steps):
                        flat[pl.ds(base + i, SUB, stride=steps), :] = cells[p, i]
                    out_ref[2 * (pair + p) + parity] = flat[base : base + width, :].astype(
                        jnp.bfloat16
                    )

        @pl.loop(0, trips)
        def _(t):
            start = jnp.minimum(t * size, pairs - size)
            first = size // 2
            chunk(start, first, 0)
            chunk(start + first, size - first, first)

        margin = halo - 1 - layer
        if margin:
            zero_row = jnp.zeros((steps + 2, SUB, chans), jnp.bfloat16)
            for end, low in ((0, 0), (1, 2 * pairs - margin)):

                @pl.when(ends_ref[end] != 0)
                def _():
                    for row in range(low, low + margin):
                        dst[row % 2, row // 2] = zero_row

        src, dst = dst, src


def convolve(ends, north, mid, south, conv_weight, conv_bias):
    layers, _, _, chans, _ = conv_weight.shape
    side, width, _ = mid.shape
    halo = north.shape[0]
    steps = width // SUB
    state = pltpu.VMEM(((2, side // 2 + halo, steps + 2, SUB, chans)), jnp.bfloat16)
    vmem = pl.BlockSpec(memory_space=pltpu.VMEM)
    return pl.pallas_call(
        conv_kernel,
        in_specs=[pl.BlockSpec(memory_space=pltpu.SMEM)] + [vmem] * 5,
        out_specs=vmem,
        out_shape=jax.ShapeDtypeStruct(mid.shape, jnp.bfloat16),
        scratch_shapes=[
            pltpu.VMEM((layers, 12 * chans, 2 * chans), jnp.bfloat16),
            state,
            state,
            pltpu.VMEM((16 * width, chans), jnp.float32),
        ],
        compiler_params=pltpu.CompilerParams(vmem_limit_bytes=VMEM_LIMIT),
        name="convolve",
    )(ends, north, mid, south, conv_weight, conv_bias)


def on_device(
    fine, parent, coverage, owner_slot, w_query, w_key, w_value, norm_gain, conv_weight, conv_bias
):
    side, width, chans = fine.shape
    tile_cols = width // side
    layers = conv_weight.shape[0]
    position = lax.axis_index("row")
    count = lax.axis_size("row")
    local_cov = lax.dynamic_slice_in_dim(coverage, position * tile_cols, tile_cols, 0)
    slots = jnp.take(owner_slot, local_cov.reshape(-1), axis=0)
    f32 = jnp.float32
    keys = jnp.dot(parent[0], w_key, preferred_element_type=f32).astype(jnp.bfloat16)
    keys = jnp.einsum("kd,cd->kc", keys, w_query, preferred_element_type=f32)
    keys = (keys * (LOG2E / chans**0.5)).astype(jnp.bfloat16)
    values = jnp.dot(parent[0], w_value, preferred_element_type=f32).astype(jnp.bfloat16)
    all_kv = lax.all_gather(jnp.concatenate([keys, values], axis=1), "row", axis=0)
    mixed = attend(fine, all_kv, slots, norm_gain, tile_cols)
    north = lax.ppermute(mixed[side - layers :], "row", [(i, i + 1) for i in range(count - 1)])
    south = lax.ppermute(mixed[:layers], "row", [(i + 1, i) for i in range(count - 1)])
    ends = jnp.stack([position == 0, position == count - 1]).astype(jnp.int32)
    return convolve(ends, north, mixed, south, conv_weight, conv_bias)


def solution(mesh):
    spread = P(("groups", "row"), None, None)
    placed = (spread, spread, P("groups", None), P("groups")) + (P(),) * 6
    return jax.shard_map(
        on_device, mesh=mesh, in_specs=placed, out_specs=spread, check_vma=False
    )
```

profile of v0, /device:TPU:1, one launch (start us, length us, event | category | flops | bytes accessed | tf_op | source)
XLA Modules:
  0.0 118.1 jit_solution(16598882662662725580)
XLA Ops:
  6.5 0.0 copy-start
  6.5 0.0 all-gather.3.cloned.1.call-start
  6.5 0.9 copy-done
  7.5 1.1 convolution_convert_fusion
  8.6 1.3 %fusion = bf16[256,128]{0,1:T(8,128)(2,1)S(1)} fusion(bf16[128,128]{1,0:T(8,128)(2,1)} %param.14, bf16[512,128]{1,0:T(8,128)(2,1)} %param.15, bf16[1,256,512]{2,1,0:T(8,128)(2,1)S(1)} %copy-done), kind=kOutput, calls=%fused_computation.4 | convolution fusion | flops 42041344 | bytes 491520 | tf_op jit(solution)/shard_map/kd,cd->kc/dot_general | solution.py:221
  9.9 0.7 pad_maximum_fusion
  10.6 0.0 all-gather.3.cloned.1.call-update
  10.6 0.8 constant_dynamic-slice_fusion
  11.4 0.1 copy.14
  11.5 0.1 reshape.43
  11.5 0.1 reshape.42
  11.6 1.3 %gather_fusion = s32[8]{0:T(128)S(1)} fusion(s32[16]{0:T(128)} %param.13, s32[1024]{0:T(1024)S(1)} %pad_clamp_fusion), kind=kCustom, calls=%fused_computation | custom fusion | bytes 96 | tf_op jit(solution)/shard_map/jit(_take)/gather | solution.py:218
  12.9 0.6 and_select_fusion.slots_ref
  13.5 40.9 %all-gather.3.cloned.1.call-done = bf16[4096,256]{0,1:T(8,128)(2,1)} async-done(((bf16[256,256]{0,1:T(8,128)(2,1)}), bf16[4096,256]{0,1:T(8,128)(2,1)}) %all-gather.3.cloned.1.call-update) | async-done | bytes 2097168 | tf_op jit(solution)/shard_map/all_gather | solution.py:224
  54.5 4.1 %copy.16 = bf16[4096,256]{1,0:T(8,128)(2,1)} copy(bf16[4096,256]{0,1:T(8,128)(2,1)} %all-gather.3.cloned.1.call-done) | data formatting | bytes 4194304 | tf_op jit(solution)/shard_map/all_gather | solution.py:224
  58.5 20.3 %attend.1.mid_ref = bf16[64,128,128]{2,1,0:T(8,128)(2,1)} custom-call(s32[8]{0:T(128)} %and_select_fusion.slots_ref, bf16[64,128,128]{2,1,0:T(8,128)(2,1)} %fine_ref.1, bf16[16,256,256]{2,1,0:T(8,128)(2,1)} %bitcast.15, bf16[16,256,256]{2,1,0:T(8,128)(2,1)} %bitcast.16, bf16[16,256,256]{2,1,0:T(8,128)(2,1)} %bitcast.17, bf16[16,256,256]{2,1,0:T(8,128)(2,1)} %bitcast.18, ...), custom_call_target="tpu_custom_call" | custom-call | tf_op jit(solution)/shard_map/attend/pallas_call | solution.py:58
  78.9 1.0 fusion.5
  79.8 2.2 %collective-permute-start.1 = (bf16[4,128,128]{2,1,0:T(8,128)(2,1)S(1)}, bf16[4,128,128]{2,1,0:T(8,128)(2,1)S(1)}, u32[]{:S(2)}, u32[]{:S(2)}) collective-permute-start(bf16[4,128,128]{2,1,0:T(8,128)(2,1)S(1)} %get-tuple-element.5), channel_id=1, source_target_pairs={{1,0},{2,1},{3,2},{4,3},{5,4},{6,5},{7,6},{8,7},{9,8},{10,9},{11,1... | collective-permute-start | bytes 393224 | tf_op jit(solution)/shard_map/ppermute | solution.py:227
  82.0 3.4 %collective-permute-start = (bf16[4,128,128]{2,1,0:T(8,128)(2,1)S(1)}, bf16[4,128,128]{2,1,0:T(8,128)(2,1)S(1)}, u32[]{:S(2)}, u32[]{:S(2)}) collective-permute-start(bf16[4,128,128]{2,1,0:T(8,128)(2,1)S(1)} %get-tuple-element.6), channel_id=1, source_target_pairs={{0,1},{1,2},{2,3},{3,4},{4,5},{5,6},{6,7},{7,8},{8,9},{9,10},{10,1... | collective-permute-start | bytes 393224 | tf_op jit(solution)/shard_map/ppermute | solution.py:226
  85.4 0.7 add_convert_fusion.ends_ref
  86.1 0.0 collective-permute-done.1.south_ref
  86.1 1.3 %collective-permute-done.north_ref = bf16[4,128,128]{2,1,0:T(8,128)(2,1)S(1)} collective-permute-done((bf16[4,128,128]{2,1,0:T(8,128)(2,1)S(1)}, bf16[4,128,128]{2,1,0:T(8,128)(2,1)S(1)}, u32[]{:S(2)}, u32[]{:S(2)}) %collective-permute-start) | collective-permute-done | bytes 131104 | tf_op jit(solution)/shard_map/ppermute | solution.py:226
  87.4 0.6 copy-done.2
  88.1 23.2 %convolve.1 = bf16[64,128,128]{2,1,0:T(8,128)(2,1)} custom-call(s32[2]{0:T(128)} %add_convert_fusion.ends_ref, bf16[4,128,128]{2,1,0:T(8,128)(2,1)} %copy-done.2, bf16[64,128,128]{2,1,0:T(8,128)(2,1)} %attend.1.mid_ref, bf16[4,128,128]{2,1,0:T(8,128)(2,1)} %copy-done.1, bf16[4,3,3,128,128]{4,3,2,1,0:T(8,128)(2,1)} %w_ref.1, f32[4,128]{1,0:T(4,128)} %b_ref.1), custom_call_target="tpu_custom_call" | custom-call | tf_op jit(solution)/shard_map/convolve/pallas_call | solution.py:193
  (5 shorter events, 0.0 us)
Async XLA Ops:
  6.5 1.0 copy-start
  6.5 47.9 %all-gather.3.cloned.1.call-start = ((), (), s32[]{:S(2)}) async-start(), calls=%async_computation | async-start | bytes 2228224 | tf_op jit(solution)/shard_map/all_gather | solution.py:224
  79.8 6.3 %collective-permute-start.1 = (bf16[4,128,128]{2,1,0:T(8,128)(2,1)S(1)}, bf16[4,128,128]{2,1,0:T(8,128)(2,1)S(1)}, u32[]{:S(2)}, u32[]{:S(2)}) collective-permute-start(bf16[4,128,128]{2,1,0:T(8,128)(2,1)S(1)} %get-tuple-element.5), channel_id=1, source_target_pairs={{1,0},{2,1},{3,2},{4,3},{5,4},{6,5},{7,6},{8,7},{9,8},{10,9},{11,1... | collective-permute-start | bytes 393224 | tf_op jit(solution)/shard_map/ppermute | solution.py:227
  82.0 5.4 %collective-permute-start = (bf16[4,128,128]{2,1,0:T(8,128)(2,1)S(1)}, bf16[4,128,128]{2,1,0:T(8,128)(2,1)S(1)}, u32[]{:S(2)}, u32[]{:S(2)}) collective-permute-start(bf16[4,128,128]{2,1,0:T(8,128)(2,1)S(1)} %get-tuple-element.6), channel_id=1, source_target_pairs={{0,1},{1,2},{2,3},{3,4},{4,5},{5,6},{6,7},{7,8},{8,9},{9,10},{10,1... | collective-permute-start | bytes 393224 | tf_op jit(solution)/shard_map/ppermute | solution.py:226
  86.1 1.3 %copy-start.1 = (bf16[4,128,128]{2,1,0:T(8,128)(2,1)}, bf16[4,128,128]{2,1,0:T(8,128)(2,1)S(1)}, u32[]{:S(2)}) copy-start(bf16[4,128,128]{2,1,0:T(8,128)(2,1)S(1)} %collective-permute-done.1.south_ref) | copy-start | bytes 393220
  87.4 0.7 copy-start.2
Sparse Core Ops, SparseCore 0:
  10.7 43.6 all-gather.2
where the time goes:
time: 120 us; the launch traced here: 118 us
  Pallas kernels  43.5 us (36%)
  waiting for transfers between devices  42.3 us (35%)
  between operations  13.4 us (11%)
  local copies, waits for them, and re-layouts  8.97 us (7%)
  starting transfers between devices  5.56 us (5%)
  matrix products  2.42 us (2%)
  other arithmetic  1.94 us (2%)
    all_gather x1, waiting for transfers between devices, on_device(): lax.all_gather(jnp.concatenate([keys, values], axis=1), 'row', axis=0)  40.9 us
    pallas_call x1, Pallas kernels, convolve(): pl.pallas_call(conv_kernel, in_specs=[pl.BlockSpec(memory_space=pltpu.SME...  23.2 us
    pallas_call x1, Pallas kernels, attend(): pl.pallas_call(functools.partial(attend_kernel, cover_n, 1e-06), grid_spe...  20.3 us
    all_gather x1, local copies, waits for them, and re-layouts, on_device(): lax.all_gather(jnp.concatenate([keys, values], axis=1), 'row', axis=0)  4.06 us
    ppermute x1, starting transfers between devices, on_device(): lax.ppermute(mixed[side - layers:], 'row', [(i, i + 1) for i in range(cou...  3.4 us
  transfers between devices with their start and end apart: 3, of which 2 were waited for; matrix products, arithmetic and copies ran while one was open for 3% of the time, Pallas kernels for 0%

commit v1 on v0

v1 whole, which is shorter than its diff:
```python
import functools

import jax
import jax.numpy as jnp
from jax import lax
from jax.experimental import pallas as pl
from jax.experimental.pallas import tpu as pltpu
from jax.sharding import PartitionSpec as P

SUB = 16
LOG2E = 1.4426950408889634
VMEM_LIMIT = 56 * 1024 * 1024
MESH = pl.DeviceIdType.MESH


def flip(z, m):
    bit = 1
    while bit <= m:
        if m & bit:
            z = z + bit - 2 * bit * lax.rem(lax.div(z, bit), 2)
        bit *= 2
    return z


def gather_kernel(
    lines,
    fine_ref,
    parent_ref,
    wq_ref,
    wk_ref,
    wv_ref,
    keys_ref,
    values_ref,
    north_ref,
    south_ref,
    own_k,
    own_v,
    local_sem,
    send_sem,
    recv_sem,
    halo_send,
    halo_recv,
):
    me = lax.axis_index("row")
    count = 4 * lines
    core, col, line = lax.rem(me, 2), lax.rem(lax.div(me, 2), 2), lax.div(me, 4)
    side, halo, chans = fine_ref.shape[0], north_ref.shape[0], wq_ref.shape[0]
    others = [flip(line, m) for m in range(lines)]
    sibling = me + 1 - 2 * core
    across = me + 2 - 4 * col
    along = [z * 4 + col * 2 + core for z in others]
    beyond = [z * 4 + (1 - col) * 2 + core for z in others]
    ring_next, ring_prev = lax.rem(me + 1, count), lax.rem(me + count - 1, count)
    outer = lax.rem(me + 2 * core - 1 + count, count)

    barrier = pltpu.get_barrier_semaphore()
    peers = along[1:] + [across, sibling, outer]
    for peer in peers:
        pl.semaphore_signal(barrier, inc=1, device_id={"row": peer}, device_id_type=MESH)

    parent = parent_ref[0]
    f32 = jnp.float32
    keys = jnp.dot(parent, wk_ref[...], preferred_element_type=f32).astype(jnp.bfloat16)
    keys = lax.dot_general(wq_ref[...], keys, (((1,), (1,)), ((), ())), preferred_element_type=f32)
    own_k[...] = (keys * (LOG2E / chans**0.5)).astype(jnp.bfloat16)
    values = jnp.dot(parent, wv_ref[...], preferred_element_type=f32)
    own_v[...] = values.astype(jnp.bfloat16)
    pl.semaphore_wait(barrier, len(peers))

    held = (keys_ref, values_ref)
    sent = []

    def send(kind, block, peer, src=None):
        copy = pltpu.make_async_remote_copy(
            src_ref=held[kind].at[block] if src is None else src,
            dst_ref=held[kind].at[block],
            send_sem=send_sem.at[len(sent)],
            recv_sem=recv_sem.at[kind, block],
            device_id={"row": peer},
            device_id_type=MESH,
        )
        copy.start()
        sent.append(copy)

    def arrived(kind, block):
        pltpu.make_async_remote_copy(
            src_ref=held[kind].at[block],
            dst_ref=held[kind].at[block],
            send_sem=send_sem.at[0],
            recv_sem=recv_sem.at[kind, block],
            device_id={"row": sibling},
            device_id_type=MESH,
        ).wait_recv()

    for kind, own in enumerate((own_k, own_v)):
        for peer in [across] + along[1:] + [sibling]:
            send(kind, me, peer, own)
    local = [
        pltpu.make_async_copy(own, held[kind].at[me], local_sem.at[kind])
        for kind, own in enumerate((own_k, own_v))
    ]
    edges = [
        pltpu.make_async_remote_copy(
            src_ref=fine_ref.at[pl.ds(first, halo)],
            dst_ref=dst,
            send_sem=halo_send.at[i],
            recv_sem=halo_recv.at[i],
            device_id={"row": peer},
            device_id_type=MESH,
        )
        for i, (first, dst, peer) in enumerate(
            ((side - halo, north_ref, ring_next), (0, south_ref, ring_prev))
        )
    ]
    for copy in local + edges:
        copy.start()

    steps = [("beyond", 0)]
    for m in range(1, lines):
        steps += [("along", m), ("beyond", m)]
    if lines > 1:
        steps[0], steps[1] = steps[1], steps[0]
    for where, m in steps:
        for kind in range(2):
            block = along[m] if where == "along" else beyond[m]
            arrived(kind, block)
            if where == "along":
                send(kind, block, across)
            send(kind, block, sibling)
    for m in range(lines):
        for block in (along[m], beyond[m]):
            for kind in range(2):
                arrived(kind, block + 1 - 2 * core)
    for copy in sent:
        copy.wait_send()
    for copy in local + edges:
        copy.wait()


def gather(fine, parent, w_query, w_key, w_value, count, halo):
    _, width, chans = fine.shape
    key_rows = parent.shape[1]
    lines = count // 4
    vmem, anywhere = pl.BlockSpec(memory_space=pltpu.VMEM), pl.BlockSpec(memory_space=pl.ANY)
    bf16 = jnp.bfloat16
    edge = jax.ShapeDtypeStruct((halo, width, chans), bf16)
    dma = pltpu.SemaphoreType.DMA
    return pl.pallas_call(
        functools.partial(gather_kernel, lines),
        in_specs=[anywhere] + [vmem] * 4,
        out_specs=[anywhere] * 4,
        out_shape=[
            jax.ShapeDtypeStruct((count, chans, key_rows), bf16),
            jax.ShapeDtypeStruct((count, key_rows, chans), bf16),
            edge,
            edge,
        ],
        scratch_shapes=[
            pltpu.VMEM((chans, key_rows), bf16),
            pltpu.VMEM((key_rows, chans), bf16),
            dma((2,)),
            dma((2 * (count - 1),)),
            dma((2, count)),
            dma((2,)),
            dma((2,)),
        ],
        compiler_params=pltpu.CompilerParams(collective_id=0, has_side_effects=True),
        name="gather",
    )(fine, parent, w_query, w_key, w_value)


def edge_columns(first, last):
    lane = lax.broadcasted_iota(jnp.int32, first.shape, first.ndim - 2)
    axis = first.ndim - 2
    west = jnp.where(lane == 0, 0.0, pltpu.roll(last, 1, axis))
    east = jnp.where(lane == SUB - 1, 0.0, pltpu.roll(first, SUB - 1, axis))
    return west, east


def step_kernel(
    tile_cols,
    cover_ref,
    owner_ref,
    fine_ref,
    north_ref,
    south_ref,
    keys_ref,
    values_ref,
    gain_ref,
    w_ref,
    b_ref,
    out_ref,
    tile_k,
    tile_v,
    scores_a,
    scores_b,
    mixed,
    wide,
    state_a,
    state_b,
    flat,
):
    layers, _, _, chans, _ = w_ref.shape
    side, width, _ = fine_ref.shape
    steps = width // SUB
    halo = north_ref.shape[0]
    batch = flat.shape[0] // width
    position, count = lax.axis_index("row"), keys_ref.shape[0]
    key_rows = values_ref.shape[1]
    span = width // tile_cols
    rows_at_once = scores_a.shape[0] // span

    def fill(tile_row, k):
        for j in range(cover_ref.shape[1]):
            slot = owner_ref[cover_ref[tile_row * tile_cols + k, j]]
            rows = slice(j * key_rows, (j + 1) * key_rows)
            tile_k[:, rows] = keys_ref[slot]
            tile_v[rows, :chans] = values_ref[slot]

    def cells_of(src, row, k):
        block = src[pl.ds(row, rows_at_once), k * span : (k + 1) * span]
        return block.reshape(rows_at_once * span, chans)

    def score(src, row, k, dst):
        dst[...] = jnp.dot(cells_of(src, row, k), tile_k[...], preferred_element_type=jnp.float32)

    def blend(src, row, k, scores, at):
        top = jnp.max(scores[...], axis=-1, keepdims=True)
        weights = jnp.exp2(scores[...] - top).astype(jnp.bfloat16)
        summed = jnp.dot(weights, tile_v[...], preferred_element_type=jnp.float32)
        attended = summed[:, :chans] / summed[:, chans:]
        meansq = jnp.mean(attended * attended, axis=-1, keepdims=True)
        cells = cells_of(src, row, k).astype(jnp.float32)
        new = cells + gain_ref[...] * attended * lax.rsqrt(meansq + 1e-06)
        mixed[pl.ds(at + row, rows_at_once), k * span : (k + 1) * span] = new.astype(
            jnp.bfloat16
        ).reshape(rows_at_once, span, chans)

    tile_v[...] = jnp.ones_like(tile_v)
    above, below = jnp.maximum(position - 1, 0), jnp.minimum(position + 1, count - 1)
    for src, tile_row, at in ((north_ref, above, 0), (south_ref, below, halo + side)):
        for k in range(tile_cols):
            fill(tile_row, k)
            score(src, 0, k, scores_a)
            blend(src, 0, k, scores_a, at)
    for k in range(tile_cols):
        fill(position, k)
        score(fine_ref, 0, k, scores_a)

        @pl.loop(0, side, step=2 * rows_at_once)
        def _(row):
            middle = row + rows_at_once
            score(fine_ref, middle, k, scores_b)
            blend(fine_ref, row, k, scores_a, halo)
            score(fine_ref, jnp.minimum(middle + rows_at_once, side - rows_at_once), k, scores_a)
            blend(fine_ref, middle, k, scores_b, halo)

    at_end = (position == 0, position == count - 1)
    for end, low in ((0, 0), (1, halo + side)):

        @pl.when(at_end[end])
        def _():
            mixed[low : low + halo] = jnp.zeros((halo, width, chans), jnp.bfloat16)

    def put(dst, parity, pair, num, cells):
        west, east = edge_columns(cells[:, 0], cells[:, steps - 1])
        dst[parity, pl.ds(pair, num), 1 : steps + 1] = cells.astype(jnp.bfloat16)
        dst[parity, pl.ds(pair, num), 0] = west.astype(jnp.bfloat16)
        dst[parity, pl.ds(pair, num), steps + 1] = east.astype(jnp.bfloat16)

    def take_rows(src, src_row, pair, num):
        rows = src[pl.ds(src_row, 2 * num)].astype(jnp.float32)
        flat[0 : 2 * num * width] = rows.reshape(2 * num * width, chans)
        for parity in range(2):
            for p in range(num):
                base = (2 * p + parity) * width
                cells = jnp.stack(
                    [flat[pl.ds(base + i, SUB, stride=steps), :] for i in range(steps)]
                )
                put(state_a, parity, pair + p, 1, cells[None])

    @pl.loop(0, (side + 2 * halo) // 8)
    def _(c):
        take_rows(mixed, c * 8, c * 4, 4)

    for layer in range(layers):
        for dx in range(3):
            for r in range(4):
                for o in range(2):
                    dy = r - o
                    at = (dx * 4 + r) * chans
                    if 0 <= dy <= 2:
                        block = w_ref[layer, dy, dx] * jnp.bfloat16(0.5)
                    else:
                        block = jnp.zeros((chans, chans), jnp.bfloat16)
                    wide[layer, at : at + chans, o * chans : (o + 1) * chans] = block

    src, dst = state_a, state_b
    for layer in range(layers):
        pairs = (side + 2 * (halo - 1 - layer)) // 2
        trips = -(-pairs // 8)
        size = -(-pairs // trips)
        bias = b_ref[layer] * 0.5
        bias = jnp.concatenate([bias, bias])[None, :]
        last = layer == layers - 1

        def chunk(pair, num, slot):
            lhs = jnp.concatenate(
                [
                    src[parity, pl.ds(pair + off, num), dx : dx + steps].reshape(num * width, chans)
                    for dx in range(3)
                    for off in range(2)
                    for parity in range(2)
                ],
                axis=1,
            )
            h = jnp.dot(lhs, wide[layer], preferred_element_type=jnp.float32) + bias
            h = h + h * jnp.tanh(h)
            for parity in range(2):
                cells = h[:, parity * chans : (parity + 1) * chans].reshape(num, steps, SUB, chans)
                if not last:
                    put(dst, parity, pair, num, cells)
                    continue
                for p in range(num):
                    base = ((slot + p) * 2 + parity) * width
                    for i in range(steps):
                        flat[pl.ds(base + i, SUB, stride=steps), :] = cells[p, i]
                    out_ref[2 * (pair + p) + parity] = flat[base : base + width, :].astype(
                        jnp.bfloat16
                    )

        @pl.loop(0, trips)
        def _(t):
            start = jnp.minimum(t * size, pairs - size)
            first = size // 2
            chunk(start, first, 0)
            chunk(start + first, size - first, first)

        margin = halo - 1 - layer
        if margin:
            zero_row = jnp.zeros((steps + 2, SUB, chans), jnp.bfloat16)
            for end, low in ((0, 0), (1, 2 * pairs - margin)):

                @pl.when(at_end[end])
                def _():
                    for row in range(low, low + margin):
                        dst[row % 2, row // 2] = zero_row

        src, dst = dst, src


def step(fine, north, south, all_keys, all_values, coverage, owner_slot, gain, weight, bias):
    layers, _, _, chans, _ = weight.shape
    side, width, _ = fine.shape
    halo = north.shape[0]
    tile_cols = width // side
    keys = coverage.shape[1] * all_values.shape[1]
    at_once = halo * side
    bf16, f32 = jnp.bfloat16, jnp.float32
    state = pltpu.VMEM((2, side // 2 + halo, width // SUB + 2, SUB, chans), bf16)
    vmem, smem = pl.BlockSpec(memory_space=pltpu.VMEM), pl.BlockSpec(memory_space=pltpu.SMEM)
    return pl.pallas_call(
        functools.partial(step_kernel, tile_cols),
        in_specs=[smem] * 2 + [vmem] * 8,
        out_specs=vmem,
        out_shape=jax.ShapeDtypeStruct(fine.shape, bf16),
        scratch_shapes=[
            pltpu.VMEM((chans, keys), bf16),
            pltpu.VMEM((keys, 2 * chans), bf16),
            pltpu.VMEM((at_once, keys), f32),
            pltpu.VMEM((at_once, keys), f32),
            pltpu.VMEM((side + 2 * halo, width, chans), bf16),
            pltpu.VMEM((layers, 12 * chans, 2 * chans), bf16),
            state,
            state,
            pltpu.VMEM((16 * width, chans), f32),
        ],
        compiler_params=pltpu.CompilerParams(vmem_limit_bytes=VMEM_LIMIT),
        name="step",
    )(
        coverage,
        owner_slot,
        fine,
        north,
        south,
        all_keys,
        all_values,
        gain.reshape(1, chans),
        weight,
        bias,
    )


def on_device(
    fine, parent, coverage, owner_slot, w_query, w_key, w_value, norm_gain, conv_weight, conv_bias
):
    count, halo = lax.axis_size("row"), conv_weight.shape[0]
    keys, values, north, south = gather(fine, parent, w_query, w_key, w_value, count, halo)
    return step(
        fine, north, south, keys, values, coverage, owner_slot, norm_gain, conv_weight, conv_bias
    )


def solution(mesh):
    spread = P(("groups", "row"), None, None)
    placed = (spread, spread, P("groups", None), P("groups")) + (P(),) * 6
    return jax.shard_map(
        on_device, mesh=mesh, in_specs=placed, out_specs=spread, check_vma=False
    )
```

time: 120 us -> 71.2 us (0.59)
  waiting for transfers between devices: 42.3 us -> 0 us
  Pallas kernels: 43.5 us -> 69 us
  between operations: 13.4 us -> 0.01 us
  local copies, waits for them, and re-layouts: 8.97 us -> 1.36 us
  starting transfers between devices: 5.56 us -> 0 us
  matrix products: 2.42 us -> 0 us
  other arithmetic: 1.94 us -> 0 us
    all_gather x1 -> x0, waiting for transfers between devices: 40.9 us -> none  [on_device(): lax.all_gather(jnp.concatenate([keys, values], axis=1), 'row', axis=0)]
    pallas_call x2, Pallas kernels: 43.5 us -> 69 us  [the longest x1 40.1 us: step(): pl.pallas_call(functools.partial(step_kernel, tile_cols), in_specs=[smem]...]
    ppermute x2 -> x0, starting transfers between devices: 5.56 us -> none  [the longest x1 3.4 us: on_device(): lax.ppermute(mixed[side - layers:], 'row', [(i, i + 1) for i in range(cou...]
    all_gather x1 -> x0, local copies, waits for them, and re-layouts: 4.06 us -> none  [on_device(): lax.all_gather(jnp.concatenate([keys, values], axis=1), 'row', axis=0)]
    dot_general x2 -> x0, matrix products: 2.42 us -> none  [the longest x1 1.28 us: on_device(): keys = jnp.einsum('kd,cd->kc', keys, w_query, preferred_element_type=f32)]
    ppermute x2 -> x0, waiting for transfers between devices: 1.35 us -> none  [the longest x1 1.31 us: on_device(): lax.ppermute(mixed[side - layers:], 'row', [(i, i + 1) for i in range(cou...]
    gather x1 -> x0, local copies, waits for them, and re-layouts: 1.3 us -> none  [on_device(): slots = jnp.take(owner_slot, local_cov.reshape(-1), axis=0)]
  transfers between devices with their start and end apart: 3 -> 0, of which waited for: 2 -> 0; matrix products, arithmetic and copies ran while one was open for 3% -> 0% of each run, Pallas kernels for 0% -> 0%
where the time goes in v1:
time: 71.2 us; the launch traced here: 70.4 us
  Pallas kernels  69 us (97%)
  local copies, waits for them, and re-layouts  1.36 us (2%)
    pallas_call x1, Pallas kernels, step(): pl.pallas_call(functools.partial(step_kernel, tile_cols), in_specs=[smem]...  40.1 us
    pallas_call x1, Pallas kernels, gather(): pl.pallas_call(functools.partial(gather_kernel, lines), in_specs=[anywher...  28.9 us

profile of v1, /device:TPU:1, one launch (start us, length us, event | category | flops | bytes accessed | tf_op | source)
XLA Modules:
  0.0 70.4 jit_solution(18252683546005823760)
XLA Ops:
  0.0 1.4 %copy.11.cover_ref = s32[32,4]{1,0:T(8,128)} copy(s32[32,4]{0,1:T(4,128)} %param.12) | data formatting | bytes 1024 | tf_op args[2]
  1.4 28.9 %gather.1 = (bf16[16,128,256]{2,1,0:T(8,128)(2,1)}, bf16[16,256,128]{2,1,0:T(8,128)(2,1)}, bf16[4,128,128]{2,1,0:T(8,128)(2,1)}, bf16[4,128,128]{2,1,0:T(8,128)(2,1)}) custom-call(bf16[64,128,128]{2,1,0:T(8,128)(2,1)} %fine_ref.3, bf16[1,256,512]{2,1,0:T(8,128)(2,1)} %parent_ref.1, bf16[128,128]{1,0:T(8,128)(2,1)} %wq_ref.1, bf16[512,128]{1,0:T(8,128)(2,1)} %wk_ref.1, ...), custom_call_target="tpu_custom_call" | custom-call | tf_op jit(solution)/shard_map/gather/pallas_call | solution.py:148
  30.3 40.1 %step.1 = bf16[64,128,128]{2,1,0:T(8,128)(2,1)} custom-call(s32[32,4]{1,0:T(8,128)} %copy.11.cover_ref, s32[16]{0:T(128)} %owner_ref.1, bf16[64,128,128]{2,1,0:T(8,128)(2,1)} %fine_ref.3, bf16[4,128,128]{2,1,0:T(8,128)(2,1)} %get-tuple-element.9.north_ref, bf16[4,128,128]{2,1,0:T(8,128)(2,1)} %get-tuple-element.10.south_ref, ...), custom_call_target="tpu_custom_call" | custom-call | tf_op jit(solution)/shard_map/step/pallas_call | solution.py:362

commit v2 on v1

v2 whole, which is shorter than its diff:
```python
import functools

import jax
import jax.numpy as jnp
from jax import lax
from jax.experimental import pallas as pl
from jax.experimental.pallas import tpu as pltpu
from jax.sharding import PartitionSpec as P

SUB = 16
LOG2E = 1.4426950408889634
VMEM_LIMIT = 40 * 1024 * 1024
MESH = pl.DeviceIdType.MESH


def gather_kernel(
    lines,
    fine_ref,
    parent_ref,
    wq_ref,
    wk_ref,
    wv_ref,
    keys_ref,
    values_ref,
    north_ref,
    south_ref,
    own_k,
    own_v,
    local_sem,
    send_sem,
    recv_sem,
    halo_send,
    halo_recv,
):
    me = lax.axis_index("row")
    count = 4 * lines
    core, col, line = lax.rem(me, 2), lax.rem(lax.div(me, 2), 2), lax.div(me, 4)
    side, halo, chans = fine_ref.shape[0], north_ref.shape[0], wq_ref.shape[0]
    sibling = me + 1 - 2 * core
    across = me + 2 - 4 * col
    ring_next, ring_prev = lax.rem(me + 1, count), lax.rem(me + count - 1, count)
    outer = lax.rem(me + 2 * core - 1 + count, count)
    up = (line < lines - 1, me + 4)
    down = (line > 0, me - 4)

    barrier = pltpu.get_barrier_semaphore()
    for peer in (across, sibling, outer):
        pl.semaphore_signal(barrier, inc=1, device_id={"row": peer}, device_id_type=MESH)
    for exists, peer in (up, down):

        @pl.when(exists)
        def _():
            pl.semaphore_signal(barrier, inc=1, device_id={"row": peer}, device_id_type=MESH)

    parent = parent_ref[0]
    f32 = jnp.float32
    keys = jnp.dot(parent, wk_ref[...], preferred_element_type=f32).astype(jnp.bfloat16)
    keys = lax.dot_general(wq_ref[...], keys, (((1,), (1,)), ((), ())), preferred_element_type=f32)
    own_k[...] = (keys * (LOG2E / chans**0.5)).astype(jnp.bfloat16)
    values = jnp.dot(parent, wv_ref[...], preferred_element_type=f32)
    own_v[...] = values.astype(jnp.bfloat16)
    inside = jnp.minimum(line, 1) + jnp.minimum(lines - 1 - line, 1)
    pl.semaphore_wait(barrier, 3 + inside)

    held = (keys_ref, values_ref)
    owned = (own_k, own_v)

    def copy_of(way, kind, block, turn, peer, own=False):
        return pltpu.make_async_remote_copy(
            src_ref=owned[kind] if own else held[kind].at[block],
            dst_ref=held[kind].at[block],
            send_sem=send_sem.at[way, kind, turn],
            recv_sem=recv_sem.at[kind, block],
            device_id={"row": peer},
            device_id_type=MESH,
        )

    def arrived(kind, block):
        copy_of(3, kind, block, 0, sibling).wait_recv()

    for kind in range(2):
        for way, (exists, peer) in enumerate((up, down)):

            @pl.when(exists)
            def _():
                copy_of(way, kind, me, 0, peer, True).start()

        copy_of(2, kind, me, 0, across, True).start()
    for kind in range(2):
        copy_of(3, kind, me, 0, sibling, True).start()
    local = [pltpu.make_async_copy(owned[k], held[k].at[me], local_sem.at[k]) for k in range(2)]
    edges = [
        pltpu.make_async_remote_copy(
            src_ref=fine_ref.at[pl.ds(first, halo)],
            dst_ref=dst,
            send_sem=halo_send.at[i],
            recv_sem=halo_recv.at[i],
            device_id={"row": peer},
            device_id_type=MESH,
        )
        for i, (first, dst, peer) in enumerate(
            ((side - halo, north_ref, ring_next), (0, south_ref, ring_prev))
        )
    ]
    for copy in local:
        copy.start()

    for t in range(lines):
        for kind in range(2):
            if t:
                for way, (exists, peer) in enumerate((up, down)):
                    block = me - 4 * t if way == 0 else me + 4 * t

                    @pl.when(line >= t if way == 0 else line < lines - t)
                    def _():
                        arrived(kind, block)

                        @pl.when(exists)
                        def _():
                            copy_of(way, kind, block, t, peer).start()

                        copy_of(2, kind, block, 2 * t + way, across).start()
                        copy_of(3, kind, block, 4 * t + way, sibling).start()

        for kind in range(2):
            for way in range(2 if t else 1):
                source = across - 4 * t if way == 0 else across + 4 * t

                @pl.when(line >= t if way == 0 else line < lines - t)
                def _():
                    arrived(kind, source)
                    copy_of(3, kind, source, 4 * t + 2 + way, sibling).start()

    for copy in edges:
        copy.start()

    for t in range(lines):
        for way in range(2 if t else 1):
            shift = -4 * t if way == 0 else 4 * t

            @pl.when(line >= t if way == 0 else line < lines - t)
            def _():
                for kind in range(2):
                    arrived(kind, sibling + shift)
                    arrived(kind, sibling + (across - me) + shift)
                    copy_of(2, kind, me, 2 * t + way, across).wait_send()
                    copy_of(3, kind, me, 4 * t + way, sibling).wait_send()
                    copy_of(3, kind, me, 4 * t + 2 + way, sibling).wait_send()

        for way, (exists, peer) in enumerate((up, down)):
            has = line >= t if way == 0 else line < lines - t

            @pl.when(jnp.logical_and(has, exists))
            def _():
                for kind in range(2):
                    copy_of(way, kind, me, t, peer).wait_send()

    for copy in local + edges:
        copy.wait()


def gather(fine, parent, w_query, w_key, w_value, count, halo):
    _, width, chans = fine.shape
    key_rows = parent.shape[1]
    lines = count // 4
    vmem, anywhere = pl.BlockSpec(memory_space=pltpu.VMEM), pl.BlockSpec(memory_space=pl.ANY)
    bf16 = jnp.bfloat16
    edge = jax.ShapeDtypeStruct((halo, width, chans), bf16)
    dma = pltpu.SemaphoreType.DMA
    return pl.pallas_call(
        functools.partial(gather_kernel, lines),
        in_specs=[anywhere] + [vmem] * 4,
        out_specs=[vmem] * 2 + [anywhere] * 2,
        out_shape=[
            jax.ShapeDtypeStruct((count, chans, key_rows), bf16),
            jax.ShapeDtypeStruct((count, key_rows, chans), bf16),
            edge,
            edge,
        ],
        scratch_shapes=[
            pltpu.VMEM((chans, key_rows), bf16),
            pltpu.VMEM((key_rows, chans), bf16),
            dma((2,)),
            dma((4, 2, 4 * lines)),
            dma((2, count)),
            dma((2,)),
            dma((2,)),
        ],
        compiler_params=pltpu.CompilerParams(
            collective_id=0, has_side_effects=True, vmem_limit_bytes=16 * 1024 * 1024
        ),
        name="gather",
    )(fine, parent, w_query, w_key, w_value)


def edge_columns(first, last):
    lane = lax.broadcasted_iota(jnp.int32, first.shape, first.ndim - 2)
    axis = first.ndim - 2
    west = jnp.where(lane == 0, 0.0, pltpu.roll(last, 1, axis))
    east = jnp.where(lane == SUB - 1, 0.0, pltpu.roll(first, SUB - 1, axis))
    return west, east


def step_kernel(
    tile_cols,
    cover_ref,
    owner_ref,
    fine_ref,
    north_ref,
    south_ref,
    keys_ref,
    values_ref,
    gain_ref,
    w_ref,
    b_ref,
    out_ref,
    tile_k,
    tile_v,
    scores_a,
    scores_b,
    weights_a,
    weights_b,
    mixed,
    wide,
    state_a,
    state_b,
    flat,
    acc_a,
    acc_b,
    sems,
):
    layers, _, _, chans, _ = w_ref.shape
    side, width, _ = fine_ref.shape
    steps = width // SUB
    halo = north_ref.shape[0]
    position, count = lax.axis_index("row"), keys_ref.shape[0]
    key_rows = values_ref.shape[1]
    span = width // tile_cols
    cells = halo * span
    blocks = (side + 2 * halo) // halo
    chunks = tile_cols * blocks

    loads = [
        pltpu.make_async_copy(src, mixed.at[pl.ds(at, src.shape[0])], sems.at[i])
        for i, (src, at) in enumerate(
            ((north_ref, 0), (fine_ref, halo), (south_ref, halo + side))
        )
    ]
    for copy in loads:
        copy.start()
    above, below = jnp.maximum(position - 1, 0), jnp.minimum(position + 1, count - 1)
    for k in range(tile_cols):
        for place, tile_row in enumerate((above, position, below)):
            for j in range(cover_ref.shape[1]):
                slot = owner_ref[cover_ref[tile_row * tile_cols + k, j]]
                rows = slice(j * key_rows, (j + 1) * key_rows)
                tile_k[3 * k + place, :, rows] = keys_ref[slot]
                tile_v[3 * k + place, rows, :chans] = values_ref[slot]
                tile_v[3 * k + place, rows, chans:] = jnp.ones((key_rows, chans), jnp.bfloat16)
    for copy in loads:
        copy.wait()

    def place_of(c):
        k, block = lax.div(c, blocks), lax.rem(c, blocks)
        tile = 3 * k + jnp.minimum(block, 1) + jnp.maximum(block - (blocks - 2), 0)
        return tile, pl.ds(block * halo, halo), pl.ds(pl.multiple_of(k * span, span), span)

    def score(c, dst):
        tile, rows, cols = place_of(c)
        mine = mixed[rows, cols].reshape(cells, chans)
        dst[...] = jnp.dot(mine, tile_k[tile], preferred_element_type=jnp.float32)

    def soften(src, dst):
        for at in range(0, cells, 32):
            some = src[at : at + 32]
            top = jnp.max(some, axis=-1, keepdims=True)
            dst[at : at + 32] = jnp.exp2(some - top).astype(jnp.bfloat16)

    def blend(c, weights):
        tile, rows, cols = place_of(c)
        summed = jnp.dot(weights[...], tile_v[tile], preferred_element_type=jnp.float32)
        attended = summed[:, :chans] / summed[:, chans:]
        meansq = jnp.mean(attended * attended, axis=-1, keepdims=True)
        mine = mixed[rows, cols].reshape(cells, chans).astype(jnp.float32)
        new = mine + gain_ref[...] * attended * lax.rsqrt(meansq + 1e-06)
        mixed[rows, cols] = new.astype(jnp.bfloat16).reshape(halo, span, chans)

    score(0, scores_a)
    score(1, scores_b)
    soften(scores_a, weights_a)

    @pl.loop(1, chunks - 1, step=2)
    def _(c):
        score(c + 1, scores_a)
        soften(scores_b, weights_b)
        blend(c - 1, weights_a)
        score(c + 2, scores_b)
        soften(scores_a, weights_a)
        blend(c, weights_b)

    soften(scores_b, weights_b)
    blend(chunks - 2, weights_a)
    blend(chunks - 1, weights_b)

    at_end = (position == 0, position == count - 1)
    for end, low in ((0, 0), (1, halo + side)):

        @pl.when(at_end[end])
        def _():
            mixed[low : low + halo] = jnp.zeros((halo, width, chans), jnp.bfloat16)

    def put(dst, parity, pair, num, cells):
        west, east = edge_columns(cells[:, 0], cells[:, steps - 1])
        dst[parity, pl.ds(pair, num), 1 : steps + 1] = cells.astype(jnp.bfloat16)
        dst[parity, pl.ds(pair, num), 0] = west.astype(jnp.bfloat16)
        dst[parity, pl.ds(pair, num), steps + 1] = east.astype(jnp.bfloat16)

    def take_rows(src, src_row, pair, num):
        rows = src[pl.ds(src_row, 2 * num)].astype(jnp.float32)
        flat[0 : 2 * num * width] = rows.reshape(2 * num * width, chans)
        for parity in range(2):
            for p in range(num):
                base = (2 * p + parity) * width
                cells = jnp.stack(
                    [flat[pl.ds(base + i, SUB, stride=steps), :] for i in range(steps)]
                )
                put(state_a, parity, pair + p, 1, cells[None])

    @pl.loop(0, (side + 2 * halo) // 8)
    def _(c):
        take_rows(mixed, c * 8, c * 4, 4)

    for layer in range(layers):
        for dx in range(3):
            for r in range(4):
                for o in range(2):
                    dy = r - o
                    at = (dx * 4 + r) * chans
                    if 0 <= dy <= 2:
                        block = w_ref[layer, dy, dx] * jnp.bfloat16(0.5)
                    else:
                        block = jnp.zeros((chans, chans), jnp.bfloat16)
                    wide[layer, at : at + chans, o * chans : (o + 1) * chans] = block

    src, dst = state_a, state_b
    for layer in range(layers):
        pairs = (side + 2 * (halo - 1 - layer)) // 2
        last = layer == layers - 1
        size = min((4, 5), key=lambda n: (-(-pairs // n) * n, -n))
        trips = -(-pairs // size)
        bias = b_ref[layer] * 0.5
        bias = jnp.concatenate([bias, bias])[None, :]

        def first_of(t):
            return jnp.minimum(t * size, pairs - size)

        def multiply(t, acc):
            pair = first_of(t)
            lhs = jnp.concatenate(
                [
                    src[parity, pl.ds(pair + off, size), dx : dx + steps].reshape(
                        size * width, chans
                    )
                    for dx in range(3)
                    for off in range(2)
                    for parity in range(2)
                ],
                axis=1,
            )
            acc[: size * width] = jnp.dot(lhs, wide[layer], preferred_element_type=jnp.float32)

        def activate(t, acc, base):
            pair = first_of(t)
            for p in range(size):
                h = acc[p * width : (p + 1) * width] + bias
                h = h + h * jnp.tanh(h)
                for parity in range(2):
                    cells = h[:, parity * chans : (parity + 1) * chans]
                    cells = cells.reshape(1, steps, SUB, chans)
                    if not last:
                        put(dst, parity, pair + p, 1, cells)
                        continue
                    at = base + (2 * p + parity) * width
                    for i in range(steps):
                        flat[pl.ds(at + i, SUB, stride=steps), :] = cells[0, i]
                    out_ref[2 * (pair + p) + parity] = flat[at : at + width, :].astype(
                        jnp.bfloat16
                    )

        multiply(0, acc_a)

        @pl.loop(0, (trips - 1) // 2)
        def _(t):
            multiply(2 * t + 1, acc_b)
            activate(2 * t, acc_a, 0)
            multiply(2 * t + 2, acc_a)
            activate(2 * t + 1, acc_b, 2 * size * width)

        if trips % 2 == 0:
            multiply(trips - 1, acc_b)
            activate(trips - 2, acc_a, 0)
            activate(trips - 1, acc_b, 2 * size * width)
        else:
            activate(trips - 1, acc_a, 0)

        margin = halo - 1 - layer
        if margin:
            zero_row = jnp.zeros((steps + 2, SUB, chans), jnp.bfloat16)
            for end, low in ((0, 0), (1, 2 * pairs - margin)):

                @pl.when(at_end[end])
                def _():
                    for row in range(low, low + margin):
                        dst[row % 2, row // 2] = zero_row

        src, dst = dst, src


def step(fine, north, south, all_keys, all_values, coverage, owner_slot, gain, weight, bias):
    layers, _, _, chans, _ = weight.shape
    side, width, _ = fine.shape
    halo = north.shape[0]
    tile_cols = width // side
    keys = coverage.shape[1] * all_values.shape[1]
    at_once = halo * side
    bf16, f32 = jnp.bfloat16, jnp.float32
    state = pltpu.VMEM((2, side // 2 + halo, width // SUB + 2, SUB, chans), bf16)
    vmem, smem = pl.BlockSpec(memory_space=pltpu.VMEM), pl.BlockSpec(memory_space=pltpu.SMEM)
    return pl.pallas_call(
        functools.partial(step_kernel, tile_cols),
        in_specs=[smem] * 2 + [pl.BlockSpec(memory_space=pl.ANY)] * 3 + [vmem] * 5,
        out_specs=vmem,
        out_shape=jax.ShapeDtypeStruct(fine.shape, bf16),
        scratch_shapes=[
            pltpu.VMEM((3 * tile_cols, chans, keys), bf16),
            pltpu.VMEM((3 * tile_cols, keys, 2 * chans), bf16),
            pltpu.VMEM((at_once, keys), f32),
            pltpu.VMEM((at_once, keys), f32),
            pltpu.VMEM((at_once, keys), bf16),
            pltpu.VMEM((at_once, keys), bf16),
            pltpu.VMEM((side + 2 * halo, width, chans), bf16),
            pltpu.VMEM((layers, 12 * chans, 2 * chans), bf16),
            state,
            state,
            pltpu.VMEM((20 * width, chans), f32),
            pltpu.VMEM((5 * width, 2 * chans), f32),
            pltpu.VMEM((5 * width, 2 * chans), f32),
            pltpu.SemaphoreType.DMA((3,)),
        ],
        compiler_params=pltpu.CompilerParams(vmem_limit_bytes=VMEM_LIMIT),
        name="step",
    )(
        coverage,
        owner_slot,
        fine,
        north,
        south,
        all_keys,
        all_values,
        gain.reshape(1, chans),
        weight,
        bias,
    )


def on_device(
    fine, parent, coverage, owner_slot, w_query, w_key, w_value, norm_gain, conv_weight, conv_bias
):
    count, halo = lax.axis_size("row"), conv_weight.shape[0]
    keys, values, north, south = gather(fine, parent, w_query, w_key, w_value, count, halo)
    return step(
        fine, north, south, keys, values, coverage, owner_slot, norm_gain, conv_weight, conv_bias
    )


def solution(mesh):
    spread = P(("groups", "row"), None, None)
    placed = (spread, spread, P("groups", None), P("groups")) + (P(),) * 6
    return jax.shard_map(
        on_device, mesh=mesh, in_specs=placed, out_specs=spread, check_vma=False
    )
```

time: 71.2 us -> 76.2 us (1.070)
  local copies, waits for them, and re-layouts: 1.36 us -> 7.19 us
    unnamed x1 -> x21, local copies, waits for them, and re-layouts: 1.36 us -> 7.19 us
    pallas_call x1, Pallas kernels: 28.9 us -> 27.6 us  [gather(): pl.pallas_call(functools.partial(gather_kernel, lines), in_specs=[anywher...]
    pallas_call x1, Pallas kernels: 40.1 us -> 41 us  [step(): pl.pallas_call(functools.partial(step_kernel, tile_cols), in_specs=[smem]...]
where the time goes in v2:
time: 76.2 us; the launch traced here: 75.8 us
  Pallas kernels  68.6 us (90%)
  local copies, waits for them, and re-layouts  7.19 us (9%)
    pallas_call x1, Pallas kernels, step(): pl.pallas_call(functools.partial(step_kernel, tile_cols), in_specs=[smem]...  41 us
    pallas_call x1, Pallas kernels, gather(): pl.pallas_call(functools.partial(gather_kernel, lines), in_specs=[anywher...  27.6 us
    unnamed x21, local copies, waits for them, and re-layouts  7.19 us

profile of v2, /device:TPU:1, one launch (start us, length us, event | category | flops | bytes accessed | tf_op | source)
XLA Modules:
  0.0 75.8 jit_solution(11838736307572451009)
XLA Ops:
  0.0 0.0 copy-start.7
  0.0 0.0 copy-start.9
  0.0 0.0 copy-start.8
  0.0 0.8 %copy.11.cover_ref = s32[32,4]{1,0:T(8,128)S(1)} copy(s32[32,4]{0,1:T(4,128)} %param.12) | data formatting | bytes 1024 | tf_op args[2]
  0.8 0.0 copy-start
  0.8 1.6 %copy-done = bf16[64,128,128]{2,1,0:T(8,128)(2,1)S(1)} copy-done((bf16[64,128,128]{2,1,0:T(8,128)(2,1)S(1)}, bf16[64,128,128]{2,1,0:T(8,128)(2,1)}, u32[]{:S(2)}) %copy-start) | copy-done | bytes 2097176
  2.4 0.0 copy-start.3
  2.4 0.9 %copy-done.3 = bf16[1,256,512]{2,1,0:T(8,128)(2,1)S(1)} copy-done((bf16[1,256,512]{2,1,0:T(8,128)(2,1)S(1)}, bf16[1,256,512]{2,1,0:T(8,128)(2,1)}, u32[]{:S(2)}) %copy-start.3) | copy-done | bytes 262168
  3.4 0.0 copy-start.4
  3.4 0.9 %copy-done.4 = bf16[512,128]{1,0:T(8,128)(2,1)S(1)} copy-done((bf16[512,128]{1,0:T(8,128)(2,1)S(1)}, bf16[512,128]{1,0:T(8,128)(2,1)}, u32[]{:S(2)}) %copy-start.4) | copy-done | bytes 131096
  4.3 0.0 copy-start.5
  4.3 0.9 %copy-done.5 = bf16[512,128]{1,0:T(8,128)(2,1)S(1)} copy-done((bf16[512,128]{1,0:T(8,128)(2,1)S(1)}, bf16[512,128]{1,0:T(8,128)(2,1)}, u32[]{:S(2)}) %copy-start.5) | copy-done | bytes 131096
  5.2 0.0 copy-start.6
  5.2 0.8 copy-done.6
  5.9 0.0 copy-start.1
  5.9 27.6 %gather.1 = (bf16[16,128,256]{2,1,0:T(8,128)(2,1)S(1)}, bf16[16,256,128]{2,1,0:T(8,128)(2,1)S(1)}, bf16[4,128,128]{2,1,0:T(8,128)(2,1)S(1)}, bf16[4,128,128]{2,1,0:T(8,128)(2,1)S(1)}) custom-call(bf16[64,128,128]{2,1,0:T(8,128)(2,1)S(1)} %copy-done, bf16[1,256,512]{2,1,0:T(8,128)(2,1)S(1)} %copy-done.3, bf16[128,128]{1,0:T(8,128)(2,1)S(1)} %copy-done.6, ...), custom_call_target="tpu_custom_call" | custom-call | tf_op jit(solution)/shard_map/gather/pallas_call | solution.py:170
  33.5 0.0 copy-done.7
  33.5 0.0 copy-done.9
  33.6 0.0 copy-done.8
  33.6 0.0 copy-done.1
  33.6 0.0 copy-start.2
  33.6 1.3 %copy-done.2 = bf16[4,3,3,128,128]{4,3,2,1,0:T(8,128)(2,1)S(1)} copy-done((bf16[4,3,3,128,128]{4,3,2,1,0:T(8,128)(2,1)S(1)}, bf16[4,3,3,128,128]{4,3,2,1,0:T(8,128)(2,1)}, u32[]{:S(2)}) %copy-start.2) | copy-done | bytes 1179672
  34.8 41.0 %step.1 = bf16[64,128,128]{2,1,0:T(8,128)(2,1)} custom-call(s32[32,4]{1,0:T(8,128)S(1)} %copy.11.cover_ref, s32[16]{0:T(128)S(1)} %copy-done.8, bf16[64,128,128]{2,1,0:T(8,128)(2,1)S(1)} %copy-done.1, bf16[4,128,128]{2,1,0:T(8,128)(2,1)S(1)} %get-tuple-element.9.north_ref, bf16[4,128,128]{2,1,0:T(8,128)(2,1)S(1)} %get-tuple-element.10.south_ref, ...), custom_call_target="tpu_custom_call" | custom-call | tf_op jit(solution)/shard_map/step/pallas_call | solution.py:429
Async XLA Ops:
  0.0 33.5 %copy-start.7 = (f32[4,128]{1,0:T(4,128)S(1)}, f32[4,128]{1,0:T(4,128)}, u32[]{:S(2)}) copy-start(f32[4,128]{1,0:T(4,128)} %b_ref.1) | copy-start | bytes 6148
  0.0 33.5 %copy-start.9 = (f32[128]{0:T(128)S(1)}, f32[128]{0:T(128)}, u32[]{:S(2)}) copy-start(f32[128]{0:T(128)} %param.17) | copy-start | bytes 1540
  0.0 33.5 %copy-start.8 = (s32[16]{0:T(128)S(1)}, s32[16]{0:T(128)}, u32[]{:S(2)}) copy-start(s32[16]{0:T(128)} %owner_ref.1) | copy-start | bytes 196
  0.8 1.6 %copy-start = (bf16[64,128,128]{2,1,0:T(8,128)(2,1)S(1)}, bf16[64,128,128]{2,1,0:T(8,128)(2,1)}, u32[]{:S(2)}) copy-start(bf16[64,128,128]{2,1,0:T(8,128)(2,1)} %fine_ref.3) | copy-start | bytes 6291460
  2.4 0.9 %copy-start.3 = (bf16[1,256,512]{2,1,0:T(8,128)(2,1)S(1)}, bf16[1,256,512]{2,1,0:T(8,128)(2,1)}, u32[]{:S(2)}) copy-start(bf16[1,256,512]{2,1,0:T(8,128)(2,1)} %parent_ref.1) | copy-start | bytes 786436
  3.4 0.9 %copy-start.4 = (bf16[512,128]{1,0:T(8,128)(2,1)S(1)}, bf16[512,128]{1,0:T(8,128)(2,1)}, u32[]{:S(2)}) copy-start(bf16[512,128]{1,0:T(8,128)(2,1)} %wk_ref.1) | copy-start | bytes 393220
  4.3 0.9 %copy-start.5 = (bf16[512,128]{1,0:T(8,128)(2,1)S(1)}, bf16[512,128]{1,0:T(8,128)(2,1)}, u32[]{:S(2)}) copy-start(bf16[512,128]{1,0:T(8,128)(2,1)} %wv_ref.1) | copy-start | bytes 393220
  5.2 0.8 copy-start.6
  5.9 27.6 %copy-start.1 = (bf16[64,128,128]{2,1,0:T(8,128)(2,1)S(1)}, bf16[64,128,128]{2,1,0:T(8,128)(2,1)}, u32[]{:S(2)}) copy-start(bf16[64,128,128]{2,1,0:T(8,128)(2,1)} %fine_ref.3) | copy-start | bytes 6291460
  33.6 1.3 %copy-start.2 = (bf16[4,3,3,128,128]{4,3,2,1,0:T(8,128)(2,1)S(1)}, bf16[4,3,3,128,128]{4,3,2,1,0:T(8,128)(2,1)}, u32[]{:S(2)}) copy-start(bf16[4,3,3,128,128]{4,3,2,1,0:T(8,128)(2,1)} %w_ref.1) | copy-start | bytes 3538948

commit v3 on v2

--- a/solution.py
+++ b/solution.py
@@ -9,7 +9,7 @@
 
 SUB = 16
 LOG2E = 1.4426950408889634
-VMEM_LIMIT = 40 * 1024 * 1024
+VMEM_LIMIT = 56 * 1024 * 1024
 MESH = pl.DeviceIdType.MESH
 
 
@@ -102,7 +102,7 @@
             ((side - halo, north_ref, ring_next), (0, south_ref, ring_prev))
         )
     ]
-    for copy in local:
+    for copy in local + edges:
         copy.start()
 
     for t in range(lines):
@@ -130,9 +130,6 @@
                 def _():
                     arrived(kind, source)
                     copy_of(3, kind, source, 4 * t + 2 + way, sibling).start()
-
-    for copy in edges:
-        copy.start()
 
     for t in range(lines):
         for way in range(2 if t else 1):
@@ -187,7 +184,7 @@
             dma((2,)),
         ],
         compiler_params=pltpu.CompilerParams(
-            collective_id=0, has_side_effects=True, vmem_limit_bytes=16 * 1024 * 1024
+            collective_id=0, has_side_effects=True, vmem_limit_bytes=VMEM_LIMIT
         ),
         name="gather",
     )(fine, parent, w_query, w_key, w_value)
@@ -236,9 +233,9 @@
     position, count = lax.axis_index("row"), keys_ref.shape[0]
     key_rows = values_ref.shape[1]
     span = width // tile_cols
-    cells = halo * span
-    blocks = (side + 2 * halo) // halo
-    chunks = tile_cols * blocks
+    deep = scores_a.shape[0] // span
+    per_tile = side // deep
+    chunks = tile_cols * per_tile
 
     loads = [
         pltpu.make_async_copy(src, mixed.at[pl.ds(at, src.shape[0])], sems.at[i])
@@ -261,46 +258,63 @@
         copy.wait()
 
     def place_of(c):
-        k, block = lax.div(c, blocks), lax.rem(c, blocks)
-        tile = 3 * k + jnp.minimum(block, 1) + jnp.maximum(block - (blocks - 2), 0)
-        return tile, pl.ds(block * halo, halo), pl.ds(pl.multiple_of(k * span, span), span)
-
-    def score(c, dst):
-        tile, rows, cols = place_of(c)
-        mine = mixed[rows, cols].reshape(cells, chans)
-        dst[...] = jnp.dot(mine, tile_k[tile], preferred_element_type=jnp.float32)
-
-    def soften(src, dst):
-        for at in range(0, cells, 32):
+        k, block = lax.div(c, per_tile), lax.rem(c, per_tile)
+        cols = pl.ds(pl.multiple_of(k * span, span), span)
+        return 3 * k + 1, pl.ds(halo + block * deep, deep), cols
+
+    def score(place, dst):
+        tile, rows, cols = place
+        mine = mixed[rows, cols]
+        mine = mine.reshape(mine.shape[0] * span, chans)
+        num = mine.shape[0]
+        dst[:num] = jnp.dot(mine, tile_k[tile], preferred_element_type=jnp.float32)
+
+    def soften(src, dst, num):
+        for at in range(0, num, 32):
             some = src[at : at + 32]
             top = jnp.max(some, axis=-1, keepdims=True)
             dst[at : at + 32] = jnp.exp2(some - top).astype(jnp.bfloat16)
 
-    def blend(c, weights):
-        tile, rows, cols = place_of(c)
-        summed = jnp.dot(weights[...], tile_v[tile], preferred_element_type=jnp.float32)
+    def blend(place, weights):
+        tile, rows, cols = place
+        mine = mixed[rows, cols]
+        mine = mine.reshape(mine.shape[0] * span, chans).astype(jnp.float32)
+        num = mine.shape[0]
+        summed = jnp.dot(weights[:num], tile_v[tile], preferred_element_type=jnp.float32)
         attended = summed[:, :chans] / summed[:, chans:]
         meansq = jnp.mean(attended * attended, axis=-1, keepdims=True)
-        mine = mixed[rows, cols].reshape(cells, chans).astype(jnp.float32)
         new = mine + gain_ref[...] * attended * lax.rsqrt(meansq + 1e-06)
-        mixed[rows, cols] = new.astype(jnp.bfloat16).reshape(halo, span, chans)
-
-    score(0, scores_a)
-    score(1, scores_b)
-    soften(scores_a, weights_a)
+        mixed[rows, cols] = new.astype(jnp.bfloat16).reshape(num // span, span, chans)
+
+    edges = [
+        (3 * k + place, slice(at, at + halo), slice(k * span, (k + 1) * span))
+        for k in range(tile_cols)
+        for place, at in ((0, 0), (2, halo + side))
+    ]
+    buffers = ((scores_a, weights_a), (scores_b, weights_b))
+    for i, place in enumerate(edges):
+        scores, weights = buffers[i % 2]
+        score(place, scores)
+        soften(scores, weights, halo * span)
+        blend(place, weights)
+
+    full = deep * span
+    score(place_of(0), scores_a)
+    score(place_of(1), scores_b)
+    soften(scores_a, weights_a, full)
 
     @pl.loop(1, chunks - 1, step=2)
     def _(c):
-        score(c + 1, scores_a)
-        soften(scores_b, weights_b)
-        blend(c - 1, weights_a)
-        score(c + 2, scores_b)
-        soften(scores_a, weights_a)
-        blend(c, weights_b)
-
-    soften(scores_b, weights_b)
-    blend(chunks - 2, weights_a)
-    blend(chunks - 1, weights_b)
+        score(place_of(c + 1), scores_a)
+        soften(scores_b, weights_b, full)
+        blend(place_of(c - 1), weights_a)
+        score(place_of(c + 2), scores_b)
+        soften(scores_a, weights_a, full)
+        blend(place_of(c), weights_b)
+
+    soften(scores_b, weights_b, full)
+    blend(place_of(chunks - 2), weights_a)
+    blend(place_of(chunks - 1), weights_b)
 
     at_end = (position == 0, position == count - 1)
     for end, low in ((0, 0), (1, halo + side)):
@@ -346,7 +360,7 @@
     for layer in range(layers):
         pairs = (side + 2 * (halo - 1 - layer)) // 2
         last = layer == layers - 1
-        size = min((4, 5), key=lambda n: (-(-pairs // n) * n, -n))
+        size = min((8, 9), key=lambda n: (-(-pairs // n) * n, -n))
         trips = -(-pairs // size)
         bias = b_ref[layer] * 0.5
         bias = jnp.concatenate([bias, bias])[None, :]
@@ -422,7 +436,7 @@
     halo = north.shape[0]
     tile_cols = width // side
     keys = coverage.shape[1] * all_values.shape[1]
-    at_once = halo * side
+    at_once = side // 4 * side
     bf16, f32 = jnp.bfloat16, jnp.float32
     state = pltpu.VMEM((2, side // 2 + halo, width // SUB + 2, SUB, chans), bf16)
     vmem, smem = pl.BlockSpec(memory_space=pltpu.VMEM), pl.BlockSpec(memory_space=pltpu.SMEM)
@@ -442,9 +456,9 @@
             pltpu.VMEM((layers, 12 * chans, 2 * chans), bf16),
             state,
             state,
-            pltpu.VMEM((20 * width, chans), f32),
-            pltpu.VMEM((5 * width, 2 * chans), f32),
-            pltpu.VMEM((5 * width, 2 * chans), f32),
+            pltpu.VMEM((36 * width, chans), f32),
+            pltpu.VMEM((9 * width, 2 * chans), f32),
+            pltpu.VMEM((9 * width, 2 * chans), f32),
             pltpu.SemaphoreType.DMA((3,)),
         ],
         compiler_params=pltpu.CompilerParams(vmem_limit_bytes=VMEM_LIMIT),

time: 76.2 us -> 68 us (0.89)
  local copies, waits for them, and re-layouts: 7.19 us -> 1.36 us
  Pallas kernels: 68.6 us -> 66.2 us
    unnamed x21 -> x1, local copies, waits for them, and re-layouts: 7.19 us -> 1.36 us
    pallas_call x1, Pallas kernels: 41 us -> 37.5 us  [step(): pl.pallas_call(functools.partial(step_kernel, tile_cols), in_specs=[smem]...]
    pallas_call x1, Pallas kernels: 27.6 us -> 28.7 us  [gather(): pl.pallas_call(functools.partial(gather_kernel, lines), in_specs=[anywher...]
where the time goes in v3:
time: 68 us; the launch traced here: 67.7 us
  Pallas kernels  66.2 us (97%)
  local copies, waits for them, and re-layouts  1.36 us (2%)
    pallas_call x1, Pallas kernels, step(): pl.pallas_call(functools.partial(step_kernel, tile_cols), in_specs=[smem]...  37.5 us
    pallas_call x1, Pallas kernels, gather(): pl.pallas_call(functools.partial(gather_kernel, lines), in_specs=[anywher...  28.7 us
    unnamed x1, local copies, waits for them, and re-layouts  1.36 us

profile of v3, /device:TPU:1, one launch (start us, length us, event | category | flops | bytes accessed | tf_op | source)
XLA Modules:
  0.0 67.7 jit_solution(10694053570444729564)
XLA Ops:
  0.0 1.4 %copy.11.cover_ref = s32[32,4]{1,0:T(8,128)} copy(s32[32,4]{0,1:T(4,128)} %param.12) | data formatting | bytes 1024 | tf_op args[2]
  1.4 28.7 %gather.1 = (bf16[16,128,256]{2,1,0:T(8,128)(2,1)}, bf16[16,256,128]{2,1,0:T(8,128)(2,1)}, bf16[4,128,128]{2,1,0:T(8,128)(2,1)}, bf16[4,128,128]{2,1,0:T(8,128)(2,1)}) custom-call(bf16[64,128,128]{2,1,0:T(8,128)(2,1)} %fine_ref.3, bf16[1,256,512]{2,1,0:T(8,128)(2,1)} %parent_ref.1, bf16[128,128]{1,0:T(8,128)(2,1)} %wq_ref.1, bf16[512,128]{1,0:T(8,128)(2,1)} %wk_ref.1, ...), custom_call_target="tpu_custom_call" | custom-call | tf_op jit(solution)/shard_map/gather/pallas_call | solution.py:167
  30.1 37.5 %step.1 = bf16[64,128,128]{2,1,0:T(8,128)(2,1)} custom-call(s32[32,4]{1,0:T(8,128)} %copy.11.cover_ref, s32[16]{0:T(128)} %owner_ref.1, bf16[64,128,128]{2,1,0:T(8,128)(2,1)} %fine_ref.3, bf16[4,128,128]{2,1,0:T(8,128)(2,1)} %get-tuple-element.9.north_ref, bf16[4,128,128]{2,1,0:T(8,128)(2,1)} %get-tuple-element.10.south_ref, ...), custom_call_target="tpu_custom_call" | custom-call | tf_op jit(solution)/shard_map/step/pallas_call | solution.py:443
